TPU v7x, 32 devices: a whole 2x2x4 slice. The times are simulated.
32 devices in a mesh: row: 4 (over y, core), col: 8 (over z, x).
Axes of the slice: x: 2, y: 2, z: 4, core: 2. Of those that a mesh axis runs over, the one named last changes fastest.
Arguments:
- noise_latents: bfloat16 [4096, 2048], P('row', 'col'), may hold values from -40 to 40
- data_latents: bfloat16 [16384, 2048], P('col', 'row'), may hold values from -6 to 6
- noise_sizes: int32 [8], replicated, may hold values from 1 to 1024, 4096 in all
- data_sizes: int32 [8], replicated, may hold values from 1 to 4096, 16384 in all
Outputs:
- velocity: float32 [4096, 2048], P('row', 'col')
- noise_potential: float32 [4096], P('row')
- data_potential: float32 [16384], P('col')
Inputs may be any that keep to these rules, and one draw needn't show every extreme that they name: `noise_sizes`: clusters take consecutive runs of noise samples in order of the cluster number; every cluster is non-empty and the largest holds exactly 1024. `data_sizes`: clusters take consecutive runs of data samples in order of the cluster number; every cluster is non-empty and the largest holds exactly 4096.
All inputs are finite; a program needn't handle non-finite values.
Results may differ from a plain program's by a relative error of at most 0.007.
Values may be sent and summed in bfloat16 or wider, within the bound.
A program may use at most 128 MiB of HBM per device.

v0:
```python
import jax
import jax.numpy as jnp
from jax import lax
from jax.sharding import PartitionSpec as P

ITERS = 3


epsilon = 0.05
masked_value = -1e30


def cluster_of(positions, cluster_sizes):
    boundaries = jnp.cumsum(cluster_sizes)[:-1]
    return jnp.sum((positions[:, None] >= boundaries[None, :]).astype(jnp.int32), axis=1)


def lse_over_cols(scores, same_cluster):
    masked = jnp.where(same_cluster, scores, masked_value)
    largest = lax.pmax(jnp.max(masked, axis=1), "col")
    totals = lax.psum(
        jnp.sum(jnp.where(same_cluster, jnp.exp(masked - largest[:, None]), 0.0), axis=1), "col"
    )
    return largest + jnp.log(totals)


def lse_over_rows(scores, same_cluster):
    masked = jnp.where(same_cluster, scores, masked_value)
    largest = lax.pmax(jnp.max(masked, axis=0), "row")
    totals = lax.psum(
        jnp.sum(jnp.where(same_cluster, jnp.exp(masked - largest[None, :]), 0.0), axis=0), "row"
    )
    return largest + jnp.log(totals)


def per_device(noise_latents, data_latents, noise_sizes, data_sizes):
    row_count = noise_latents.shape[0]
    col_count = data_latents.shape[0]
    full_width = noise_latents.shape[1] * lax.axis_size("col")
    row_positions = lax.axis_index("row") * row_count + jnp.arange(row_count, dtype=jnp.int32)
    col_positions = lax.axis_index("col") * col_count + jnp.arange(col_count, dtype=jnp.int32)
    noise_cluster = cluster_of(row_positions, noise_sizes)
    data_cluster = cluster_of(col_positions, data_sizes)
    same_cluster = noise_cluster[:, None] == data_cluster[None, :]
    data_full = lax.all_gather(data_latents, "row", axis=1, tiled=True)
    data_sq = jnp.sum(jnp.square(data_full.astype(jnp.float32)), axis=1)
    shard_piece = lax.all_gather(noise_latents, "col", axis=1, tiled=True)
    inner = lax.dot_general(
        shard_piece, data_full, (((1,), (1,)), ((), ())), preferred_element_type=jnp.float32
    )
    inner, noise_sq = (inner, jnp.sum(jnp.square(shard_piece.astype(jnp.float32)), axis=1))
    cost = (noise_sq[:, None] + data_sq[None, :] - 2.0 * inner) / full_width
    data_potential = jnp.zeros((col_count,), jnp.float32)
    noise_potential = jnp.zeros((row_count,), jnp.float32)
    for iteration in range(ITERS):
        noise_potential = -epsilon * lse_over_cols(
            (data_potential[None, :] - cost) / epsilon, same_cluster
        )
        data_potential = -epsilon * lse_over_rows(
            (noise_potential[:, None] - cost) / epsilon, same_cluster
        )
    scores = (data_potential[None, :] - cost) / epsilon
    row_lse = lse_over_cols(scores, same_cluster)
    weights = jnp.where(
        same_cluster, jnp.exp(jnp.where(same_cluster, scores, masked_value) - row_lse[:, None]), 0.0
    ).astype(jnp.bfloat16)
    partials = jnp.dot(weights, data_full, preferred_element_type=jnp.float32)
    share_width = noise_latents.shape[1]
    summed = lax.psum(partials.astype(jnp.bfloat16), "col").astype(jnp.float32)
    target = lax.dynamic_slice_in_dim(summed, lax.axis_index("col") * share_width, share_width, 1)
    velocity = target - noise_latents.astype(jnp.float32)
    return (velocity, noise_potential, data_potential)


def solution(mesh):
    placed = (P("row", "col"), P("col", "row"), P(), P())
    return jax.shard_map(
        per_device,
        mesh=mesh,
        in_specs=placed,
        out_specs=(P("row", "col"), P("row"), P("col")),
        check_vma=False,
    )
```

profile of v0, /device:TPU:0, one launch (start us, length us, event | category | flops | bytes accessed | tf_op | source)
XLA Modules:
  0.0 591.1 jit_solution(2214551199291564672)
XLA Ops:
  10.6 77.2 %all-gather.3.cloned.1.call-done = bf16[1024,2048]{1,0:T(8,128)(2,1)} async-done(((bf16[1024,256]{1,0:T(8,128)(2,1)}), bf16[1024,2048]{1,0:T(8,128)(2,1)}) %all-gather.3.cloned.1.call-update) | async-done | bytes 4194320 | tf_op jit(solution)/shard_map/all_gather | solution.py:47
  90.9 55.0 %all-gather.5.cloned.1.call-done = bf16[2048,2048]{1,0:T(8,128)(2,1)} async-done(((bf16[2048,512]{1,0:T(8,128)(2,1)}), bf16[2048,2048]{1,0:T(8,128)(2,1)}) %all-gather.5.cloned.1.call-update) | async-done | bytes 8388624 | tf_op jit(solution)/shard_map/all_gather | solution.py:45
  145.9 5.2 multiply_reduce_fusion
  151.6 14.0 %fusion.8 = (f32[1024]{0:T(1024)S(1)}, f32[1024,2048]{1,0:T(8,128)}) fusion(s32[2048]{0:T(1024)S(1)} %convert_reduce_fusion, s32[1024]{0:T(1024)S(1)} %convert_reduce_fusion.1, bf16[1024,2048]{1,0:T(8,128)(2,1)} %all-gather.3.cloned.1.call-done, bf16[2048,2048]{1,0:T(8,128)(2,1)S(1)} %copy-done, f32[2048]{0:T(1024)S(1)} %multiply_reduce_fusion, ...), kind=kOutput, calls=%fused_computation.26 | convolution fusion | flops 8608807936 | bytes 21000192 | tf_op jit(solution)/shard_map/dot_general | solution.py:48
  165.6 21.3 %pmax.49 = f32[1024]{0:T(1024)S(1)} all-reduce(f32[1024]{0:T(1024)S(1)} %get-tuple-element.3), channel_id=1, replica_groups=mesh['row'=4,'col'=8] {'col'}, use_global_device_ids=true, to_apply=%region_7.8 | all-reduce | flops 1024 | bytes 8192 | tf_op jit(solution)/shard_map/pmax | solution.py:20
  192.0 17.1 %psum.56 = f32[1024]{0:T(1024)S(1)} all-reduce(f32[1024]{0:T(1024)S(1)} %fusion), channel_id=1, replica_groups=mesh['row'=4,'col'=8] {'col'}, use_global_device_ids=true, to_apply=%region_9.10 | all-reduce | flops 1024 | bytes 8192 | tf_op jit(solution)/shard_map/psum | solution.py:21
  213.5 6.1 %pmax.50 = f32[2048]{0:T(1024)S(1)} all-reduce(f32[2048]{0:T(1024)S(1)} %fusion.9), channel_id=1, replica_groups=mesh['row'=4,'col'=8] {'row'}, use_global_device_ids=true, to_apply=%region_11.12 | all-reduce | flops 2048 | bytes 16384 | tf_op jit(solution)/shard_map/pmax | solution.py:29
  219.6 5.1 fusion.1
  224.7 6.0 %psum.57 = f32[2048]{0:T(1024)S(1)} all-reduce(f32[2048]{0:T(1024)S(1)} %fusion.1), channel_id=1, replica_groups=mesh['row'=4,'col'=8] {'row'}, use_global_device_ids=true, to_apply=%region_13.14 | all-reduce | flops 2048 | bytes 16384 | tf_op jit(solution)/shard_map/psum | solution.py:30
  235.1 19.1 %pmax.51 = f32[1024]{0:T(1024)S(1)} all-reduce(f32[1024]{0:T(1024)S(1)} %fusion.10), channel_id=1, replica_groups=mesh['row'=4,'col'=8] {'col'}, use_global_device_ids=true, to_apply=%region_15.16 | all-reduce | flops 1024 | bytes 8192 | tf_op jit(solution)/shard_map/pmax | solution.py:20
  259.4 17.1 %psum.58 = f32[1024]{0:T(1024)S(1)} all-reduce(f32[1024]{0:T(1024)S(1)} %fusion.2), channel_id=1, replica_groups=mesh['row'=4,'col'=8] {'col'}, use_global_device_ids=true, to_apply=%region_17.18 | all-reduce | flops 1024 | bytes 8192 | tf_op jit(solution)/shard_map/psum | solution.py:21
  280.8 5.8 pmax.52
  286.6 5.1 fusion.3
  291.7 6.6 %psum.59 = f32[2048]{0:T(1024)S(1)} all-reduce(f32[2048]{0:T(1024)S(1)} %fusion.3), channel_id=1, replica_groups=mesh['row'=4,'col'=8] {'row'}, use_global_device_ids=true, to_apply=%region_21.22 | all-reduce | flops 2048 | bytes 16384 | tf_op jit(solution)/shard_map/psum | solution.py:30
  302.7 19.1 %pmax.53 = f32[1024]{0:T(1024)S(1)} all-reduce(f32[1024]{0:T(1024)S(1)} %fusion.12), channel_id=1, replica_groups=mesh['row'=4,'col'=8] {'col'}, use_global_device_ids=true, to_apply=%region_23.24 | all-reduce | flops 1024 | bytes 8192 | tf_op jit(solution)/shard_map/pmax | solution.py:20
  326.9 17.2 %psum.60 = f32[1024]{0:T(1024)S(1)} all-reduce(f32[1024]{0:T(1024)S(1)} %fusion.4), channel_id=1, replica_groups=mesh['row'=4,'col'=8] {'col'}, use_global_device_ids=true, to_apply=%region_25.26 | all-reduce | flops 1024 | bytes 8192 | tf_op jit(solution)/shard_map/psum | solution.py:21
  348.4 5.8 pmax.54
  354.2 5.1 fusion.5
  359.3 6.5 %psum.61 = f32[2048]{0:T(1024)S(1)} all-reduce(f32[2048]{0:T(1024)S(1)} %fusion.5), channel_id=1, replica_groups=mesh['row'=4,'col'=8] {'row'}, use_global_device_ids=true, to_apply=%region_29.30 | all-reduce | flops 2048 | bytes 16384 | tf_op jit(solution)/shard_map/psum | solution.py:30
  370.2 19.3 %pmax.55 = f32[1024]{0:T(1024)S(1)} all-reduce(f32[1024]{0:T(1024)S(1)} %fusion.14), channel_id=1, replica_groups=mesh['row'=4,'col'=8] {'col'}, use_global_device_ids=true, to_apply=%region_31.32 | all-reduce | flops 1024 | bytes 8192 | tf_op jit(solution)/shard_map/pmax | solution.py:20
  389.6 5.1 fusion.6
  394.7 17.2 %psum.62 = f32[1024]{0:T(1024)S(1)} all-reduce(f32[1024]{0:T(1024)S(1)} %fusion.6), channel_id=1, replica_groups=mesh['row'=4,'col'=8] {'col'}, use_global_device_ids=true, to_apply=%region_33.34 | all-reduce | flops 1024 | bytes 8192 | tf_op jit(solution)/shard_map/psum | solution.py:21
  411.9 15.9 %fusion.24 = bf16[1024,2048]{1,0:T(8,128)(2,1)} fusion(bf16[2048,2048]{1,0:T(8,128)(2,1)} %all-gather.5.cloned.1.call-done, f32[1024,2048]{1,0:T(8,128)} %get-tuple-element.4, f32[1024]{0:T(1024)S(1)} %log_add_fusion, f32[2048]{0:T(1024)S(1)} %add_multiply_fusion, s32[2048]{0:T(1024)S(1)} %convert_reduce_fusion, s32[1024]{0:T(1024)S(1)} %convert_reduce_fusion.1), kind=kOutput, calls=%fused_computation.41 | convolution fusion | flops 8606711808 | bytes 20996096 | tf_op jit(solution)/shard_map/dot_general | solution.py:67
  427.8 154.7 %all-reduce.2.cloned.1.call-done = bf16[1024,2048]{1,0:T(8,128)(2,1)} async-done(((bf16[1024,2048]{1,0:T(8,128)(2,1)}), bf16[1024,2048]{1,0:T(8,128)(2,1)}) %all-reduce.2.cloned.1.call-update) | async-done | bytes 4194320 | tf_op jit(solution)/shard_map/psum | solution.py:69
  (40 shorter events, 50.4 us)
Async XLA Ops:
  7.2 80.6 %all-gather.3.cloned.1.call-start = ((), (), s32[]{:S(2)}) async-start(), calls=%async_computation | async-start | bytes 4718592 | tf_op jit(solution)/shard_map/all_gather | solution.py:47
  7.9 138.0 %all-gather.5.cloned.1.call-start = ((), (), s32[]{:S(2)}) async-start(), calls=%async_computation.1 | async-start | bytes 10485760 | tf_op jit(solution)/shard_map/all_gather | solution.py:45
  8.6 573.8 %all-reduce.2.cloned.1.call-start = ((), (), s32[]{:S(2)}) async-start(), calls=%async_computation.2 | async-start | bytes 8388608 | tf_op jit(solution)/shard_map/psum | solution.py:69
  145.9 5.8 copy-start
  344.1 15.2 %copy-start.3 = (f32[1024]{0:T(1024)}, f32[1024]{0:T(1024)S(1)}, u32[]{:S(2)}) copy-start(f32[1024]{0:T(1024)S(1)} %add_multiply_fusion.3) | copy-start | bytes 12292
  365.8 46.0 %copy-start.2 = (f32[2048]{0:T(1024)}, f32[2048]{0:T(1024)S(1)}, u32[]{:S(2)}) copy-start(f32[2048]{0:T(1024)S(1)} %add_multiply_fusion) | copy-start | bytes 24580
  411.9 170.6 %copy-start.1 = (bf16[1024,256]{1,0:T(8,128)(2,1)S(1)}, bf16[1024,256]{1,0:T(8,128)(2,1)}, u32[]{:S(2)}) copy-start(bf16[1024,256]{1,0:T(8,128)(2,1)} %param.4) | copy-start | bytes 1572868
Sparse Core Ops, SparseCore 0:
  10.0 77.7 all-gather.2
  89.3 56.4 all-gather.4
  427.9 154.5 all-reduce.1
where the time goes:
time: 592 us; the launch traced here: 591 us
  waiting for transfers between devices  288 us (49%)
  blocking collectives  184 us (31%)
  other arithmetic  74 us (12%)
  matrix products  29.9 us (5%)
  between operations  14 us (2%)
    psum x1, waiting for transfers between devices, per_device(): summed = lax.psum(partials.astype(jnp.bfloat16), 'col').astype(jnp.float32)  155 us
    pmax x4, blocking collectives, lse_over_cols(): largest = lax.pmax(jnp.max(masked, axis=1), 'col')  78.9 us
    all_gather x1, waiting for transfers between devices, per_device(): shard_piece = lax.all_gather(noise_latents, 'col', axis=1, tiled=True)  77.2 us
    psum x4, blocking collectives, lse_over_cols(): lax.psum(jnp.sum(jnp.where(same_cluster, jnp.exp(masked - largest[:, None...  68.6 us
    all_gather x1, waiting for transfers between devices, per_device(): data_full = lax.all_gather(data_latents, 'row', axis=1, tiled=True)  55 us
    reduce_sum x4, other arithmetic, lse_over_cols(): jnp.sum(jnp.where(same_cluster, jnp.exp(masked - largest[:, None]), 0.0),...  20.3 us
    psum x3, blocking collectives, lse_over_rows(): lax.psum(jnp.sum(jnp.where(same_cluster, jnp.exp(masked - largest[None, :...  19.2 us
    pmax x3, blocking collectives, lse_over_rows(): largest = lax.pmax(jnp.max(masked, axis=0), 'row')  17.6 us
  transfers between devices with their start and end apart: 3, of which 3 were waited for; matrix products, arithmetic and copies ran while one was open for 1% of the time, Pallas kernels for 0%

commit v1 on v0

v1 whole, which is shorter than its diff:
```python
import functools
import math

import jax
import jax.numpy as jnp
from jax import lax
from jax.experimental import pallas as pl
from jax.experimental.pallas import tpu as pltpu
from jax.sharding import PartitionSpec as P

ITERS = 3
EPSILON = 0.05
MASKED = -1e30
Z = 4
CORES = 2
PIECES = 4
T = 128
UNIT = EPSILON * math.log(2.0)
MESH = pl.DeviceIdType.MESH


def kernel(
    R, C, xin, yin, nsz, dsz,
    target, fout, gout,
    X, Y, S, Wt, NC, F, avec, bvec, qvec, nvec, cbuf, rbuf,
    psend, pown, xrecv, zsend, zrecv,
    local_sem, xg_send, xg_recv, yg_send, yg_recv,
    ce_send, ce_recv, re_send, re_recv, px_send, px_recv, pz_send, pz_recv,
):
    rows, wc = xin.shape
    cols, wr = yin.shape
    width = wc * C
    XN = C // Z
    YN = R // CORES
    r = lax.axis_index("row")
    c = lax.axis_index("col")
    z, x = lax.div(c, XN), lax.rem(c, XN)
    y, core = lax.div(r, CORES), lax.rem(r, CORES)
    scale = 2.0 / (width * UNIT)

    def rdma(src, dst, send, recv, **peer):
        return pltpu.make_async_remote_copy(
            src_ref=src, dst_ref=dst, send_sem=send, recv_sem=recv,
            device_id=peer, device_id_type=MESH,
        )

    barrier = pltpu.get_barrier_semaphore()
    for k in range(1, C):
        pl.semaphore_signal(barrier, inc=1, device_id={"col": lax.rem(c + k, C)}, device_id_type=MESH)
    for k in range(1, R):
        pl.semaphore_signal(barrier, inc=1, device_id={"row": lax.rem(r + k, R)}, device_id_type=MESH)
    pl.semaphore_wait(barrier, C - 1 + R - 1)

    sent = []

    def noise_part(block):
        return X.at[:, pl.ds(pl.multiple_of(block * wc, wc), wc)]

    def noise_copy(block, way, own=False):
        peer = {0: c + XN, 1: c - XN, 2: c + 1, 3: c - 1}[way]
        return rdma(xin if own else noise_part(block), noise_part(block),
                    xg_send.at[block, way], xg_recv.at[block], col=peer)

    def can_noise(way):
        return {0: z + 1 < Z, 1: z >= 1, 2: x + 1 < XN, 3: x >= 1}[way]

    def send(cond, make):
        pl.when(cond)(lambda: make().start())
        sent.append((cond, make))

    def noise_send(block, way, cond=None, own=False):
        ok = can_noise(way) if cond is None else jnp.logical_and(cond, can_noise(way))
        send(ok, lambda: noise_copy(block, way, own))

    piece = cols // PIECES

    def data_part(block, q):
        return Y.at[pl.ds(q * piece, piece), pl.ds(pl.multiple_of(block * wr, wr), wr)]

    def data_copy(block, q, way, own=False):
        peer = {0: r + CORES, 1: r - CORES, 2: r + 1 - 2 * core}[way]
        src = yin.at[pl.ds(q * piece, piece), :] if own else data_part(block, q)
        return rdma(src, data_part(block, q), yg_send.at[block, q, way], yg_recv.at[block, q], row=peer)

    def can_data(way):
        return {0: y + 1 < YN, 1: y >= 1, 2: y >= 0}[way]

    def data_send(block, q, way, cond=None, own=False):
        ok = can_data(way) if cond is None else jnp.logical_and(cond, can_data(way))
        send(ok, lambda: data_copy(block, q, way, own))

    for way in (0, 1, 2, 3):
        noise_send(c, way, own=True)
    for q in range(PIECES):
        for way in (0, 1):
            data_send(r, q, way, own=True)
    for q in range(PIECES):
        data_send(r, q, 2, own=True)
    lx = pltpu.make_async_copy(xin, noise_part(c), local_sem.at[0])
    ly = pltpu.make_async_copy(yin, Y.at[:, pl.ds(pl.multiple_of(r * wr, wr), wr)], local_sem.at[1])
    lx.start()
    ly.start()

    def cluster(position, sizes):
        total = jnp.int32(0)
        number = jnp.zeros(position.shape, jnp.int32)
        for k in range(7):
            total = total + sizes[k]
            number = number + (position >= total).astype(jnp.int32)
        return number

    for i in range(rows // T):
        NC[pl.ds(i * T, T), :] = cluster(
            r * rows + i * T + lax.broadcasted_iota(jnp.int32, (T, T), 0), nsz)

    def take_noise(dz, dx):
        here = jnp.logical_and(
            jnp.logical_and(z + dz >= 0, z + dz < Z), jnp.logical_and(x + dx >= 0, x + dx < XN))
        block = c + dz * XN + dx
        pl.when(here)(lambda: noise_copy(block, 0).wait_recv())
        if dx == 0:
            noise_send(block, 1 if dz > 0 else 0, here)
            noise_send(block, 2, here)
            noise_send(block, 3, here)
        elif abs(dx) < XN - 1:
            noise_send(block, 3 if dx > 0 else 2, here)

    def take_data(dy, q):
        here = jnp.logical_and(y + dy >= 0, y + dy < YN)
        block = r + dy * CORES
        pl.when(here)(lambda: data_copy(block, q, 0).wait_recv())
        if abs(dy) < YN - 1:
            data_send(block, q, 1 if dy > 0 else 0, here)
        data_send(block, q, 2, here)

    def signs(d):
        return (d, -d) if d else (0,)

    for step in range(1, Z + 1):
        if step < Z:
            for dz in signs(step):
                take_noise(dz, 0)
        if step <= PIECES:
            for dy in signs(1):
                take_data(dy, step - 1)
        for dz in signs(step - 1):
            for dx in signs(1):
                take_noise(dz, dx)
    for step in range(2, XN):
        for dz in range(1 - Z, Z):
            for dx in signs(step):
                take_noise(dz, dx)
    for step in range(2, YN):
        for q in range(PIECES):
            for dy in signs(step):
                take_data(dy, q)
    sibling = r + 1 - 2 * core
    for dy in range(1 - YN, YN):
        here = jnp.logical_and(y + dy >= 0, y + dy < YN)
        for q in range(PIECES):
            pl.when(here)(lambda dy=dy, q=q: data_copy(sibling + dy * CORES, q, 0).wait_recv())
    lx.wait()
    ly.wait()

    def squares(ref, i):
        total = jnp.zeros((T, T), jnp.float32)
        for k in range(width // T):
            v = ref[pl.ds(pl.multiple_of(i * T, T), T), pl.ds(k * T, T)].astype(jnp.float32)
            total = total + v * v
        return jnp.sum(total.T, axis=0, keepdims=True) * (1.0 / (width * UNIT))

    def lanes(i, n=T):
        return pl.ds(pl.multiple_of(i * n, n), n)

    @pl.loop(0, cols // (2 * T))
    def _(j):
        both = lax.dot_general(
            X[...], Y[lanes(j, 2 * T), :], (((1,), (1,)), ((), ())), preferred_element_type=jnp.float32)
        for h in range(2):
            i = j * 2 + h
            dc = cluster(c * cols + i * T + lax.broadcasted_iota(jnp.int32, (1, T), 1), dsz)
            S[:, lanes(i)] = jnp.where(NC[...] == dc, both[:, h * T:(h + 1) * T] * scale, MASKED)
            q = squares(Y, i)
            qvec[:, lanes(i)] = q
            avec[:, lanes(i)] = -q

    @pl.loop(0, rows // T)
    def _(i):
        nvec[:, lanes(i)] = squares(X, i)

    def over_cols(e):
        @pl.loop(0, rows // T)
        def _(i):
            def term(k):
                return S[lanes(i), pl.ds(k * T, T)] + avec[:, pl.ds(k * T, T)]

            top = term(0)
            for k in range(1, cols // T):
                top = jnp.maximum(top, term(k))
            total = jnp.exp2(term(0) - top)
            for k in range(1, cols // T):
                total = total + jnp.exp2(term(k) - top)
            top, total = top.T, total.T
            best = jnp.max(top, axis=0, keepdims=True)
            cbuf[e, c, 0:1, lanes(i)] = best
            cbuf[e, c, 1:2, lanes(i)] = jnp.sum(total * jnp.exp2(top - best), axis=0, keepdims=True)

    def spread(vec):
        for i in range(rows // T):
            F[pl.ds(i * T, T), :] = jnp.broadcast_to(vec[:, i * T:(i + 1) * T], (T, T)).T

    def over_rows(e):
        G = 64

        @pl.loop(0, cols // T)
        def _(k):
            def term(i):
                return S[pl.ds(i * G, G), lanes(k)] + F[pl.ds(i * G, G), :]

            top = term(0)
            for i in range(1, rows // G):
                top = jnp.maximum(top, term(i))
            total = jnp.exp2(term(0) - top)
            for i in range(1, rows // G):
                total = total + jnp.exp2(term(i) - top)
            best = jnp.max(top, axis=0, keepdims=True)
            rbuf[e, r, 0:1, lanes(k)] = best
            rbuf[e, r, 1:2, lanes(k)] = jnp.sum(total * jnp.exp2(top - best), axis=0, keepdims=True)

    def exchange(buf, send_sem, recv_sem, e, me, n, axis):
        for k in range(1, n):
            rdma(buf.at[e, me], buf.at[e, me], send_sem.at[e, k - 1], recv_sem.at[e, me],
                 **{axis: lax.rem(me + k, n)}).start()
        for k in range(1, n):
            other = lax.rem(me + k, n)
            rdma(buf.at[e, other], buf.at[e, other], send_sem.at[e, k - 1], recv_sem.at[e, other],
                 **{axis: other}).wait_recv()
        best = buf[e, 0, 0:1, :]
        for k in range(1, n):
            best = jnp.maximum(best, buf[e, k, 0:1, :])
        total = buf[e, 0, 1:2, :] * jnp.exp2(buf[e, 0, 0:1, :] - best)
        for k in range(1, n):
            total = total + buf[e, k, 1:2, :] * jnp.exp2(buf[e, k, 0:1, :] - best)
        return best + jnp.log(total) * (1.0 / math.log(2.0))

    @pl.loop(0, ITERS)
    def _(e):
        over_cols(e)
        b = -exchange(cbuf, ce_send, ce_recv, e, c, C, "col")
        bvec[...] = b
        spread(b)
        over_rows(e)
        avec[...] = -exchange(rbuf, re_send, re_recv, e, r, R, "row")

    fout[...] = (bvec[...] + nvec[...]) * UNIT
    gout[...] = (avec[...] + qvec[...]) * UNIT
    over_cols(ITERS)
    spread(exchange(cbuf, ce_send, ce_recv, ITERS, c, C, "col"))

    @pl.loop(0, cols // T)
    def _(k):
        Wt[:, lanes(k)] = jnp.exp2(S[:, lanes(k)] + avec[:, lanes(k)] - F[...]).astype(jnp.bfloat16)

    def partial_sum(part):
        return jnp.dot(Wt[...], Y[:, lanes(part, wc)], preferred_element_type=jnp.float32).astype(jnp.bfloat16)

    def px_copy(k, d):
        return rdma(psend.at[k, d - 1], xrecv.at[k, d - 1], px_send.at[k, d - 1], px_recv.at[k, d - 1],
                    col=z * XN + lax.rem(x + d, XN))

    def pz_copy(k):
        return rdma(zsend.at[k], zrecv.at[k], pz_send.at[k], pz_recv.at[k],
                    col=lax.rem(z + 1 + k, Z) * XN + x)

    @pl.loop(0, Z)
    def _(k):
        zd = lax.rem(z + 1 + k, Z)
        for d in range(1, XN):
            psend[k, d - 1] = partial_sum(zd * XN + lax.rem(x + d, XN))
            px_copy(k, d).start()
        pown[k] = partial_sum(zd * XN + x)

    def x_sum(k):
        for d in range(1, XN):
            px_copy(k, d).wait_recv()
        total = pown[k].astype(jnp.float32)
        for d in range(1, XN):
            total = total + xrecv[k, d - 1].astype(jnp.float32)
        return total

    @pl.loop(0, Z - 1)
    def _(k):
        zsend[k] = x_sum(k).astype(jnp.bfloat16)
        pz_copy(k).start()

    total = x_sum(Z - 1)
    for k in range(Z - 1):
        pz_copy(k).wait_recv()
        total = total + zrecv[k].astype(jnp.float32)
    target[...] = total

    for cond, make in sent:
        pl.when(cond)(lambda make=make: make().wait_send())
    for e in range(ITERS + 1):
        for k in range(1, C):
            rdma(cbuf.at[e, c], cbuf.at[e, c], ce_send.at[e, k - 1], ce_recv.at[e, c],
                 col=lax.rem(c + k, C)).wait_send()
    for e in range(ITERS):
        for k in range(1, R):
            rdma(rbuf.at[e, r], rbuf.at[e, r], re_send.at[e, k - 1], re_recv.at[e, r],
                 row=lax.rem(r + k, R)).wait_send()
    for k in range(Z):
        for d in range(1, XN):
            px_copy(k, d).wait_send()
    for k in range(Z - 1):
        pz_copy(k).wait_send()


def per_device(R, C, noise_latents, data_latents, noise_sizes, data_sizes):
    rows, wc = noise_latents.shape
    cols, wr = data_latents.shape
    width = wc * C
    XN = C // Z
    f32, bf16 = jnp.float32, jnp.bfloat16
    dma = pltpu.SemaphoreType.DMA
    vmem = pl.BlockSpec(memory_space=pltpu.VMEM)
    anywhere = pl.BlockSpec(memory_space=pl.ANY)
    smem = pl.BlockSpec(memory_space=pltpu.SMEM)
    target, f, g = pl.pallas_call(
        functools.partial(kernel, R, C),
        out_shape=(
            jax.ShapeDtypeStruct((rows, wc), f32),
            jax.ShapeDtypeStruct((1, rows), f32),
            jax.ShapeDtypeStruct((1, cols), f32),
        ),
        in_specs=[anywhere, anywhere, smem, smem],
        out_specs=(vmem, vmem, vmem),
        scratch_shapes=[
            pltpu.VMEM((rows, width), bf16),
            pltpu.VMEM((cols, width), bf16),
            pltpu.VMEM((rows, cols), f32),
            pltpu.VMEM((rows, cols), bf16),
            pltpu.VMEM((rows, T), jnp.int32),
            pltpu.VMEM((rows, T), f32),
            pltpu.VMEM((1, cols), f32),
            pltpu.VMEM((1, rows), f32),
            pltpu.VMEM((1, cols), f32),
            pltpu.VMEM((1, rows), f32),
            pltpu.VMEM((ITERS + 1, C, 2, rows), f32),
            pltpu.VMEM((ITERS, R, 2, cols), f32),
            pltpu.VMEM((Z, XN - 1, rows, wc), bf16),
            pltpu.VMEM((Z, rows, wc), bf16),
            pltpu.VMEM((Z, XN - 1, rows, wc), bf16),
            pltpu.VMEM((Z - 1, rows, wc), bf16),
            pltpu.VMEM((Z - 1, rows, wc), bf16),
            dma((2,)),
            dma((C, 4)),
            dma((C,)),
            dma((R, PIECES, 3)),
            dma((R, PIECES)),
            dma((ITERS + 1, C - 1)),
            dma((ITERS + 1, C)),
            dma((ITERS, R - 1)),
            dma((ITERS, R)),
            dma((Z, XN - 1)),
            dma((Z, XN - 1)),
            dma((Z - 1,)),
            dma((Z - 1,)),
        ],
        compiler_params=pltpu.CompilerParams(
            collective_id=0, has_side_effects=True, vmem_limit_bytes=58 * 1024 * 1024
        ),
        name="sinkhorn",
    )(noise_latents, data_latents, noise_sizes, data_sizes)
    velocity = target - noise_latents.astype(f32)
    return velocity, f.reshape(rows), g.reshape(cols)


def solution(mesh):
    placed = (P("row", "col"), P("col", "row"), P(), P())
    return jax.shard_map(
        functools.partial(per_device, mesh.shape["row"], mesh.shape["col"]),
        mesh=mesh,
        in_specs=placed,
        out_specs=(P("row", "col"), P("row"), P("col")),
        check_vma=False,
    )
```

time: 592 us -> 186 us (0.31)
  the two profiles are of different devices: /device:TPU:0 before, /device:TPU:13 now
where the time goes in v1:
time: 186 us
  Pallas kernels  182 us (98%)
  other arithmetic  2.3 us (1%)
    pallas_call x1, Pallas kernels, per_device(): pl.pallas_call(functools.partial(kernel, R, C), out_shape=(jax.ShapeDtype...  182 us

profile of v1, /device:TPU:13, one launch (start us, length us, event | category | flops | bytes accessed | tf_op | source)
XLA Modules:
  0.0 185.9 jit_solution(1551113422237080549)
XLA Ops:
  0.6 0.0 copy-start
  0.6 181.7 %sinkhorn.1 = (f32[1024,256]{1,0:T(8,128)}, f32[1,1024]{1,0:T(1,128)}, f32[1,2048]{1,0:T(1,128)}) custom-call(bf16[1024,256]{1,0:T(8,128)(2,1)} %xin.1, bf16[2048,512]{1,0:T(8,128)(2,1)} %yin.1, s32[8]{0:T(128)} %nsz.1, s32[8]{0:T(128)} %dsz.1), custom_call_target="tpu_custom_call" | custom-call | tf_op jit(solution)/shard_map/sinkhorn/pallas_call | solution.py:329
  182.3 0.0 copy-start.2
  182.4 0.0 copy-start.1
  182.4 0.0 copy-done
  182.4 2.3 %convert_subtract_fusion = f32[1024,256]{1,0:T(8,128)} fusion(f32[1024,256]{1,0:T(8,128)} %get-tuple-element.6, bf16[1024,256]{1,0:T(8,128)(2,1)S(1)} %copy-done), kind=kLoop, calls=%fused_computation | loop fusion | flops 524288 | bytes 2621440 | tf_op jit(solution)/shard_map/sub | solution.py:375
  184.7 0.0 copy-done.2
  184.7 0.6 copy.9
  185.3 0.0 copy-done.1
  185.3 0.6 copy.10
Async XLA Ops:
  0.6 181.7 %copy-start = (bf16[1024,256]{1,0:T(8,128)(2,1)S(1)}, bf16[1024,256]{1,0:T(8,128)(2,1)}, u32[]{:S(2)}) copy-start(bf16[1024,256]{1,0:T(8,128)(2,1)} %xin.1) | copy-start | bytes 1572868
  182.3 2.3 %copy-start.2 = (f32[1,1024]{1,0:T(1,128)S(1)}, f32[1,1024]{1,0:T(1,128)}, u32[]{:S(2)}) copy-start(f32[1,1024]{1,0:T(1,128)} %get-tuple-element.7) | copy-start | bytes 12292
  182.4 2.9 %copy-start.1 = (f32[1,2048]{1,0:T(1,128)S(1)}, f32[1,2048]{1,0:T(1,128)}, u32[]{:S(2)}) copy-start(f32[1,2048]{1,0:T(1,128)} %get-tuple-element.8) | copy-start | bytes 24580

commit v2 on v1

--- a/solution.py
+++ b/solution.py
@@ -16,16 +16,17 @@
 PIECES = 4
 T = 128
 UNIT = EPSILON * math.log(2.0)
+ORDER = ((3, 2, 1, 0), (3, 0, 2, 1), (0, 3, 1, 2), (0, 1, 2, 3))
 MESH = pl.DeviceIdType.MESH
 
 
 def kernel(
     R, C, xin, yin, nsz, dsz,
     target, fout, gout,
-    X, Y, S, Wt, NC, F, avec, bvec, qvec, nvec, cbuf, rbuf,
+    X, Y, S, Pm, Wt, NC, F, Fb, avec, bvec, qvec, nvec, cfirst, rfirst, cbuf, rbuf,
     psend, pown, xrecv, zsend, zrecv,
     local_sem, xg_send, xg_recv, yg_send, yg_recv,
-    ce_send, ce_recv, re_send, re_recv, px_send, px_recv, pz_send, pz_recv,
+    cf_send, cf_recv, rf_send, rf_recv, ce_send, ce_recv, re_send, re_recv, px_send, px_recv, pz_send, pz_recv,
 ):
     rows, wc = xin.shape
     cols, wr = yin.shape
@@ -184,11 +185,7 @@
             qvec[:, lanes(i)] = q
             avec[:, lanes(i)] = -q
 
-    @pl.loop(0, rows // T)
-    def _(i):
-        nvec[:, lanes(i)] = squares(X, i)
-
-    def over_cols(e):
+    def first_over_cols():
         @pl.loop(0, rows // T)
         def _(i):
             def term(k):
@@ -202,20 +199,16 @@
                 total = total + jnp.exp2(term(k) - top)
             top, total = top.T, total.T
             best = jnp.max(top, axis=0, keepdims=True)
-            cbuf[e, c, 0:1, lanes(i)] = best
-            cbuf[e, c, 1:2, lanes(i)] = jnp.sum(total * jnp.exp2(top - best), axis=0, keepdims=True)
-
-    def spread(vec):
-        for i in range(rows // T):
-            F[pl.ds(i * T, T), :] = jnp.broadcast_to(vec[:, i * T:(i + 1) * T], (T, T)).T
-
-    def over_rows(e):
+            cfirst[0, c, 0:1, lanes(i)] = best
+            cfirst[0, c, 1:2, lanes(i)] = jnp.sum(total * jnp.exp2(top - best), axis=0, keepdims=True)
+
+    def first_over_rows():
         G = 64
 
         @pl.loop(0, cols // T)
         def _(k):
             def term(i):
-                return S[pl.ds(i * G, G), lanes(k)] + F[pl.ds(i * G, G), :]
+                return S[pl.ds(i * G, G), lanes(k)] + Fb[pl.ds(i * G, G), :]
 
             top = term(0)
             for i in range(1, rows // G):
@@ -224,61 +217,158 @@
             for i in range(1, rows // G):
                 total = total + jnp.exp2(term(i) - top)
             best = jnp.max(top, axis=0, keepdims=True)
-            rbuf[e, r, 0:1, lanes(k)] = best
-            rbuf[e, r, 1:2, lanes(k)] = jnp.sum(total * jnp.exp2(top - best), axis=0, keepdims=True)
-
-    def exchange(buf, send_sem, recv_sem, e, me, n, axis):
-        for k in range(1, n):
+            rfirst[0, r, 0:1, lanes(k)] = best
+            rfirst[0, r, 1:2, lanes(k)] = jnp.sum(total * jnp.exp2(top - best), axis=0, keepdims=True)
+
+    def over_cols(e, out):
+        @pl.loop(0, rows // T)
+        def _(i):
+            b = Fb[lanes(i), :]
+            total = jnp.zeros((T, T), jnp.float32)
+            for k in range(cols // T):
+                v = jnp.exp2(S[lanes(i), pl.ds(k * T, T)] + avec[:, pl.ds(k * T, T)] + b)
+                out[lanes(i), pl.ds(k * T, T)] = v.astype(out.dtype)
+                total = total + v
+            cbuf[e, c, :, lanes(i)] = jnp.sum(total.T, axis=0, keepdims=True)
+
+    def over_rows(e):
+        G = 64
+
+        @pl.loop(0, cols // T)
+        def _(k):
+            total = jnp.zeros((G, T), jnp.float32)
+            for i in range(rows // G):
+                total = total + Pm[pl.ds(i * G, G), lanes(k)] * F[pl.ds(i * G, G), :]
+            rbuf[e, r, :, lanes(k)] = jnp.sum(total, axis=0, keepdims=True)
+
+    def spread(vec, use):
+        for i in range(rows // T):
+            use(pl.ds(i * T, T), jnp.broadcast_to(vec[:, i * T:(i + 1) * T], (T, T)).T)
+
+    def put(buf, send_sem, recv_sem, e, me, n, axis):
+        return [
             rdma(buf.at[e, me], buf.at[e, me], send_sem.at[e, k - 1], recv_sem.at[e, me],
-                 **{axis: lax.rem(me + k, n)}).start()
+                 **{axis: lax.rem(me + k, n)})
+            for k in range(1, n)
+        ]
+
+    def start(*group):
+        for copy in put(*group):
+            copy.start()
+
+    def arrive(buf, send_sem, recv_sem, e, me, n, axis):
         for k in range(1, n):
             other = lax.rem(me + k, n)
             rdma(buf.at[e, other], buf.at[e, other], send_sem.at[e, k - 1], recv_sem.at[e, other],
                  **{axis: other}).wait_recv()
-        best = buf[e, 0, 0:1, :]
+
+    def log2(v):
+        return jnp.log(v) * (1.0 / math.log(2.0))
+
+    def first_sum(buf, n):
+        best = buf[0, 0, 0:1, :]
         for k in range(1, n):
-            best = jnp.maximum(best, buf[e, k, 0:1, :])
-        total = buf[e, 0, 1:2, :] * jnp.exp2(buf[e, 0, 0:1, :] - best)
+            best = jnp.maximum(best, buf[0, k, 0:1, :])
+        total = buf[0, 0, 1:2, :] * jnp.exp2(buf[0, 0, 0:1, :] - best)
         for k in range(1, n):
-            total = total + buf[e, k, 1:2, :] * jnp.exp2(buf[e, k, 0:1, :] - best)
-        return best + jnp.log(total) * (1.0 / math.log(2.0))
-
-    @pl.loop(0, ITERS)
+            total = total + buf[0, k, 1:2, :] * jnp.exp2(buf[0, k, 0:1, :] - best)
+        return best + log2(total)
+
+    def plain_sum(buf, e, n):
+        total = buf[e, 0]
+        for k in range(1, n):
+            total = total + buf[e, k]
+        return total
+
+    cf = (cfirst, cf_send, cf_recv, 0, c, C, "col")
+    rf = (rfirst, rf_send, rf_recv, 0, r, R, "row")
+
+    def cg(e):
+        return (cbuf, ce_send, ce_recv, e, c, C, "col")
+
+    def rg(e):
+        return (rbuf, re_send, re_recv, e, r, R, "row")
+
+    first_over_cols()
+    start(*cf)
+
+    @pl.loop(0, rows // T)
+    def _(i):
+        nvec[:, lanes(i)] = squares(X, i)
+
+    arrive(*cf)
+    b = -first_sum(cfirst, C)
+    bvec[...] = b
+
+    def keep_b(where, v):
+        Fb[where, :] = v
+
+    spread(b, keep_b)
+    first_over_rows()
+    start(*rf)
+    arrive(*rf)
+    avec[...] = -first_sum(rfirst, R)
+
+    def step_b(where, v):
+        F[where, :] = 1.0 / v
+        Fb[where, :] = Fb[where, :] - log2(v)
+
+    @pl.loop(0, ITERS - 1)
     def _(e):
-        over_cols(e)
-        b = -exchange(cbuf, ce_send, ce_recv, e, c, C, "col")
-        bvec[...] = b
-        spread(b)
+        over_cols(e, Pm)
+        start(*cg(e))
+        arrive(*cg(e))
+        total = plain_sum(cbuf, e, C)
+        bvec[...] = bvec[...] - log2(total)
+        spread(total, step_b)
         over_rows(e)
-        avec[...] = -exchange(rbuf, re_send, re_recv, e, r, R, "row")
-
-    fout[...] = (bvec[...] + nvec[...]) * UNIT
-    gout[...] = (avec[...] + qvec[...]) * UNIT
-    over_cols(ITERS)
-    spread(exchange(cbuf, ce_send, ce_recv, ITERS, c, C, "col"))
-
-    @pl.loop(0, cols // T)
-    def _(k):
-        Wt[:, lanes(k)] = jnp.exp2(S[:, lanes(k)] + avec[:, lanes(k)] - F[...]).astype(jnp.bfloat16)
-
-    def partial_sum(part):
-        return jnp.dot(Wt[...], Y[:, lanes(part, wc)], preferred_element_type=jnp.float32).astype(jnp.bfloat16)
+        start(*rg(e))
+        arrive(*rg(e))
+        avec[...] = avec[...] - log2(plain_sum(rbuf, e, R))
+
+    over_cols(ITERS - 1, Wt)
+    start(*cg(ITERS - 1))
+
+    def order(k):
+        part = jnp.int32(0)
+        for at, row in enumerate(ORDER):
+            for step, value in enumerate(row):
+                part = part + jnp.where(jnp.logical_and(z == at, k == step), value, 0)
+        return part
+
+    def weighted(part):
+        return jnp.dot(Wt[...], Y[:, lanes(part, wc)], preferred_element_type=jnp.float32)
+
+    def scaled(v):
+        return jnp.concatenate([v[:, i * T:(i + 1) * T] * F[...] for i in range(wc // T)], axis=1).astype(jnp.bfloat16)
 
     def px_copy(k, d):
         return rdma(psend.at[k, d - 1], xrecv.at[k, d - 1], px_send.at[k, d - 1], px_recv.at[k, d - 1],
                     col=z * XN + lax.rem(x + d, XN))
 
-    def pz_copy(k):
-        return rdma(zsend.at[k], zrecv.at[k], pz_send.at[k], pz_recv.at[k],
-                    col=lax.rem(z + 1 + k, Z) * XN + x)
+    def inverse(where, v):
+        F[where, :] = 1.0 / v
+
+    head = weighted(order(0) * XN + lax.rem(x + 1, XN))
+    fout[...] = (bvec[...] + nvec[...]) * UNIT
+    gout[...] = (avec[...] + qvec[...]) * UNIT
+    arrive(*cg(ITERS - 1))
+    spread(plain_sum(cbuf, ITERS - 1, C), inverse)
+    psend[0, 0] = scaled(head)
+    px_copy(0, 1).start()
 
     @pl.loop(0, Z)
     def _(k):
-        zd = lax.rem(z + 1 + k, Z)
+        zd = order(k)
         for d in range(1, XN):
-            psend[k, d - 1] = partial_sum(zd * XN + lax.rem(x + d, XN))
-            px_copy(k, d).start()
-        pown[k] = partial_sum(zd * XN + x)
+            @pl.when(jnp.logical_or(k > 0, d > 1))
+            def _():
+                psend[k, d - 1] = scaled(weighted(zd * XN + lax.rem(x + d, XN)))
+                px_copy(k, d).start()
+
+    @pl.loop(0, Z)
+    def _(k):
+        pown[k] = scaled(weighted(order(k) * XN + x))
 
     def x_sum(k):
         for d in range(1, XN):
@@ -288,32 +378,47 @@
             total = total + xrecv[k, d - 1].astype(jnp.float32)
         return total
 
+    def pz_copy(k, to, slot):
+        return rdma(zsend.at[k], zrecv.at[slot], pz_send.at[k], pz_recv.at[slot], col=to * XN + x)
+
     @pl.loop(0, Z - 1)
     def _(k):
-        zsend[k] = x_sum(k).astype(jnp.bfloat16)
-        pz_copy(k).start()
-
-    total = x_sum(Z - 1)
-    for k in range(Z - 1):
-        pz_copy(k).wait_recv()
-        total = total + zrecv[k].astype(jnp.float32)
-    target[...] = total
+        zd = order(k)
+        right = zd > z
+        more = jnp.logical_or(jnp.logical_and(right, z > 0), jnp.logical_and(zd < z, z < Z - 1))
+        total = x_sum(k)
+
+        @pl.when(more)
+        def _():
+            pz_copy(k, z, zd).wait_recv()
+            zsend[k] = (total + zrecv[zd].astype(jnp.float32)).astype(jnp.bfloat16)
+
+        @pl.when(jnp.logical_not(more))
+        def _():
+            zsend[k] = total.astype(jnp.bfloat16)
+
+        to = jnp.where(right, z + 1, z - 1)
+        slot = jnp.where(zd == z - 1, Z, zd)
+        pz_copy(k, to, slot).start()
+
+    target[...] = x_sum(Z - 1)
+    for here, slot in ((z > 0, z), (z < Z - 1, Z)):
+        @pl.when(here)
+        def _():
+            pz_copy(0, z, slot).wait_recv()
+            target[...] += zrecv[slot].astype(jnp.float32)
 
     for cond, make in sent:
         pl.when(cond)(lambda make=make: make().wait_send())
-    for e in range(ITERS + 1):
-        for k in range(1, C):
-            rdma(cbuf.at[e, c], cbuf.at[e, c], ce_send.at[e, k - 1], ce_recv.at[e, c],
-                 col=lax.rem(c + k, C)).wait_send()
-    for e in range(ITERS):
-        for k in range(1, R):
-            rdma(rbuf.at[e, r], rbuf.at[e, r], re_send.at[e, k - 1], re_recv.at[e, r],
-                 row=lax.rem(r + k, R)).wait_send()
+    groups = [cf, rf] + [cg(e) for e in range(ITERS)] + [rg(e) for e in range(ITERS - 1)]
+    for group in groups:
+        for copy in put(*group):
+            copy.wait_send()
     for k in range(Z):
         for d in range(1, XN):
             px_copy(k, d).wait_send()
     for k in range(Z - 1):
-        pz_copy(k).wait_send()
+        pz_copy(k, z, 0).wait_send()
 
 
 def per_device(R, C, noise_latents, data_latents, noise_sizes, data_sizes):
@@ -339,33 +444,41 @@
             pltpu.VMEM((rows, width), bf16),
             pltpu.VMEM((cols, width), bf16),
             pltpu.VMEM((rows, cols), f32),
+            pltpu.VMEM((rows, cols), f32),
             pltpu.VMEM((rows, cols), bf16),
             pltpu.VMEM((rows, T), jnp.int32),
+            pltpu.VMEM((rows, T), f32),
             pltpu.VMEM((rows, T), f32),
             pltpu.VMEM((1, cols), f32),
             pltpu.VMEM((1, rows), f32),
             pltpu.VMEM((1, cols), f32),
             pltpu.VMEM((1, rows), f32),
-            pltpu.VMEM((ITERS + 1, C, 2, rows), f32),
-            pltpu.VMEM((ITERS, R, 2, cols), f32),
+            pltpu.VMEM((1, C, 2, rows), f32),
+            pltpu.VMEM((1, R, 2, cols), f32),
+            pltpu.VMEM((ITERS, C, 1, rows), f32),
+            pltpu.VMEM((ITERS - 1, R, 1, cols), f32),
             pltpu.VMEM((Z, XN - 1, rows, wc), bf16),
             pltpu.VMEM((Z, rows, wc), bf16),
             pltpu.VMEM((Z, XN - 1, rows, wc), bf16),
             pltpu.VMEM((Z - 1, rows, wc), bf16),
-            pltpu.VMEM((Z - 1, rows, wc), bf16),
+            pltpu.VMEM((Z + 1, rows, wc), bf16),
             dma((2,)),
             dma((C, 4)),
             dma((C,)),
             dma((R, PIECES, 3)),
             dma((R, PIECES)),
-            dma((ITERS + 1, C - 1)),
-            dma((ITERS + 1, C)),
-            dma((ITERS, R - 1)),
-            dma((ITERS, R)),
+            dma((1, C - 1)),
+            dma((1, C)),
+            dma((1, R - 1)),
+            dma((1, R)),
+            dma((ITERS, C - 1)),
+            dma((ITERS, C)),
+            dma((ITERS - 1, R - 1)),
+            dma((ITERS - 1, R)),
             dma((Z, XN - 1)),
             dma((Z, XN - 1)),
             dma((Z - 1,)),
-            dma((Z - 1,)),
+            dma((Z + 1,)),
         ],
         compiler_params=pltpu.CompilerParams(
             collective_id=0, has_side_effects=True, vmem_limit_bytes=58 * 1024 * 1024

time: 186 us -> 161 us (0.87)
  the two profiles are of different devices: /device:TPU:13 before, /device:TPU:0 now
where the time goes in v2:
time: 161 us
  Pallas kernels  156 us (97%)
  other arithmetic  2.3 us (1%)
    pallas_call x1, Pallas kernels, per_device(): pl.pallas_call(functools.partial(kernel, R, C), out_shape=(jax.ShapeDtype...  156 us

profile of v2, /device:TPU:0, one launch (start us, length us, event | category | flops | bytes accessed | tf_op | source)
XLA Modules:
  0.0 160.6 jit_solution(12090151867216991980)
XLA Ops:
  0.6 0.0 copy-start
  0.6 156.4 %sinkhorn.1 = (f32[1024,256]{1,0:T(8,128)}, f32[1,1024]{1,0:T(1,128)}, f32[1,2048]{1,0:T(1,128)}) custom-call(bf16[1024,256]{1,0:T(8,128)(2,1)} %xin.1, bf16[2048,512]{1,0:T(8,128)(2,1)} %yin.1, s32[8]{0:T(128)} %nsz.1, s32[8]{0:T(128)} %dsz.1), custom_call_target="tpu_custom_call" | custom-call | tf_op jit(solution)/shard_map/sinkhorn/pallas_call | solution.py:434
  157.0 0.0 copy-start.2
  157.0 0.0 copy-start.1
  157.0 0.0 copy-done
  157.1 2.3 %convert_subtract_fusion = f32[1024,256]{1,0:T(8,128)} fusion(f32[1024,256]{1,0:T(8,128)} %get-tuple-element.6, bf16[1024,256]{1,0:T(8,128)(2,1)S(1)} %copy-done), kind=kLoop, calls=%fused_computation | loop fusion | flops 524288 | bytes 2621440 | tf_op jit(solution)/shard_map/sub | solution.py:488
  159.4 0.0 copy-done.2
  159.4 0.6 copy.9
  159.9 0.0 copy-done.1
  160.0 0.6 copy.10
Async XLA Ops:
  0.6 156.4 %copy-start = (bf16[1024,256]{1,0:T(8,128)(2,1)S(1)}, bf16[1024,256]{1,0:T(8,128)(2,1)}, u32[]{:S(2)}) copy-start(bf16[1024,256]{1,0:T(8,128)(2,1)} %xin.1) | copy-start | bytes 1572868
  157.0 2.3 %copy-start.2 = (f32[1,1024]{1,0:T(1,128)S(1)}, f32[1,1024]{1,0:T(1,128)}, u32[]{:S(2)}) copy-start(f32[1,1024]{1,0:T(1,128)} %get-tuple-element.7) | copy-start | bytes 12292
  157.0 2.9 %copy-start.1 = (f32[1,2048]{1,0:T(1,128)S(1)}, f32[1,2048]{1,0:T(1,128)}, u32[]{:S(2)}) copy-start(f32[1,2048]{1,0:T(1,128)} %get-tuple-element.8) | copy-start | bytes 24580

commit v3 on v2

--- a/solution.py
+++ b/solution.py
@@ -23,7 +23,7 @@
 def kernel(
     R, C, xin, yin, nsz, dsz,
     target, fout, gout,
-    X, Y, S, Pm, Wt, NC, F, Fb, avec, bvec, qvec, nvec, cfirst, rfirst, cbuf, rbuf,
+    X, Y, S, Pm, Wt, NC, F, Fb, avec, bvec, qvec, nvec, qpart, dcvec, cfirst, rfirst, cbuf, rbuf,
     psend, pown, xrecv, zsend, zrecv,
     local_sem, xg_send, xg_recv, yg_send, yg_recv,
     cf_send, cf_recv, rf_send, rf_recv, ce_send, ce_recv, re_send, re_recv, px_send, px_recv, pz_send, pz_recv,
@@ -137,6 +137,55 @@
     def signs(d):
         return (d, -d) if d else (0,)
 
+    sibling = r + 1 - 2 * core
+
+    def take_sibling(dy, q):
+        here = jnp.logical_and(y + dy >= 0, y + dy < YN)
+        pl.when(here)(lambda: data_copy(sibling + dy * CORES, q, 0).wait_recv())
+
+    def lanes(i, n=T):
+        return pl.ds(pl.multiple_of(i * n, n), n)
+
+    def squares(ref, i, first, wide):
+        total = jnp.zeros((T, T), jnp.float32)
+        for k in range(wide // T):
+            v = ref[lanes(i), pl.ds(pl.multiple_of(first + k * T, T), T)].astype(jnp.float32)
+            total = total + v * v
+        return jnp.sum(total.T, axis=0, keepdims=True) * (1.0 / (width * UNIT))
+
+    quarter = width // Z
+    last = PIECES + 1
+    early = XN == 2 and YN == 2 and R == Z
+
+    def ready(part, q):
+        if not early:
+            return jnp.int32(last)
+        noise_step = jnp.abs(part - z) + 1
+        mine = lax.rem(part, CORES) == core
+        data_step = jnp.where(lax.div(part, CORES) == y, 1, jnp.where(mine, q + 1, q + 2))
+        return jnp.maximum(noise_step, data_step)
+
+    def tasks(step):
+        @pl.loop(0, Z * PIECES)
+        def _(t):
+            part, q = lax.div(t, PIECES), lax.rem(t, PIECES)
+
+            @pl.when(ready(part, q) == step)
+            def _():
+                features = lanes(part, quarter)
+                S[:, lanes(q, piece)] += lax.dot_general(
+                    X[:, features], Y[lanes(q, piece), features], (((1,), (1,)), ((), ())),
+                    preferred_element_type=jnp.float32)
+                for h in range(piece // T):
+                    i = q * (piece // T) + h
+                    qpart[part, :, lanes(i)] = squares(Y, i, part * quarter, quarter)
+
+    @pl.loop(0, rows // T)
+    def _(i):
+        S[lanes(i), :] = jnp.zeros((T, cols), jnp.float32)
+
+    dcvec[...] = cluster(c * cols + lax.broadcasted_iota(jnp.int32, (1, cols), 1), dsz)
+
     for step in range(1, Z + 1):
         if step < Z:
             for dz in signs(step):
@@ -147,6 +196,16 @@
         for dz in signs(step - 1):
             for dx in signs(1):
                 take_noise(dz, dx)
+        if step == 1:
+            lx.wait()
+            ly.wait()
+            for q in range(PIECES):
+                take_sibling(0, q)
+        else:
+            for dy in signs(1):
+                take_sibling(dy, step - 2)
+        if early:
+            tasks(step)
     for step in range(2, XN):
         for dz in range(1 - Z, Z):
             for dx in signs(step):
@@ -155,35 +214,18 @@
         for q in range(PIECES):
             for dy in signs(step):
                 take_data(dy, q)
-    sibling = r + 1 - 2 * core
-    for dy in range(1 - YN, YN):
-        here = jnp.logical_and(y + dy >= 0, y + dy < YN)
+    for dy in signs(1):
+        take_sibling(dy, PIECES - 1)
+    for step in range(2, YN):
         for q in range(PIECES):
-            pl.when(here)(lambda dy=dy, q=q: data_copy(sibling + dy * CORES, q, 0).wait_recv())
-    lx.wait()
-    ly.wait()
-
-    def squares(ref, i):
-        total = jnp.zeros((T, T), jnp.float32)
-        for k in range(width // T):
-            v = ref[pl.ds(pl.multiple_of(i * T, T), T), pl.ds(k * T, T)].astype(jnp.float32)
-            total = total + v * v
-        return jnp.sum(total.T, axis=0, keepdims=True) * (1.0 / (width * UNIT))
-
-    def lanes(i, n=T):
-        return pl.ds(pl.multiple_of(i * n, n), n)
-
-    @pl.loop(0, cols // (2 * T))
-    def _(j):
-        both = lax.dot_general(
-            X[...], Y[lanes(j, 2 * T), :], (((1,), (1,)), ((), ())), preferred_element_type=jnp.float32)
-        for h in range(2):
-            i = j * 2 + h
-            dc = cluster(c * cols + i * T + lax.broadcasted_iota(jnp.int32, (1, T), 1), dsz)
-            S[:, lanes(i)] = jnp.where(NC[...] == dc, both[:, h * T:(h + 1) * T] * scale, MASKED)
-            q = squares(Y, i)
-            qvec[:, lanes(i)] = q
-            avec[:, lanes(i)] = -q
+            for dy in signs(step):
+                take_sibling(dy, q)
+    tasks(last)
+    total = qpart[0]
+    for part in range(1, Z):
+        total = total + qpart[part]
+    qvec[...] = total
+    avec[...] = -total
 
     def first_over_cols():
         @pl.loop(0, rows // T)
@@ -191,9 +233,13 @@
             def term(k):
                 return S[lanes(i), pl.ds(k * T, T)] + avec[:, pl.ds(k * T, T)]
 
-            top = term(0)
-            for k in range(1, cols // T):
-                top = jnp.maximum(top, term(k))
+            number = NC[lanes(i), :]
+            top = jnp.full((T, T), MASKED, jnp.float32)
+            for k in range(cols // T):
+                at = pl.ds(k * T, T)
+                v = jnp.where(number == dcvec[:, at], S[lanes(i), at] * scale, MASKED)
+                S[lanes(i), at] = v
+                top = jnp.maximum(top, v + avec[:, at])
             total = jnp.exp2(term(0) - top)
             for k in range(1, cols // T):
                 total = total + jnp.exp2(term(k) - top)
@@ -294,7 +340,7 @@
 
     @pl.loop(0, rows // T)
     def _(i):
-        nvec[:, lanes(i)] = squares(X, i)
+        nvec[:, lanes(i)] = squares(X, i, 0, width)
 
     arrive(*cf)
     b = -first_sum(cfirst, C)
@@ -453,6 +499,8 @@
             pltpu.VMEM((1, rows), f32),
             pltpu.VMEM((1, cols), f32),
             pltpu.VMEM((1, rows), f32),
+            pltpu.VMEM((Z, 1, cols), f32),
+            pltpu.VMEM((1, cols), jnp.int32),
             pltpu.VMEM((1, C, 2, rows), f32),
             pltpu.VMEM((1, R, 2, cols), f32),
             pltpu.VMEM((ITERS, C, 1, rows), f32),

time: 161 us -> 156 us (0.969)
  Pallas kernels: 156 us -> 152 us
    pallas_call x1, Pallas kernels: 156 us -> 152 us  [per_device(): pl.pallas_call(functools.partial(kernel, R, C), out_shape=(jax.ShapeDtype...]
where the time goes in v3:
time: 156 us
  Pallas kernels  152 us (97%)
  other arithmetic  2.3 us (1%)
    pallas_call x1, Pallas kernels, per_device(): pl.pallas_call(functools.partial(kernel, R, C), out_shape=(jax.ShapeDtype...  152 us

profile of v3, /device:TPU:0, one launch (start us, length us, event | category | flops | bytes accessed | tf_op | source)
XLA Modules:
  0.0 155.7 jit_solution(6359535968139784356)
XLA Ops:
  0.6 0.0 copy-start
  0.6 151.6 %sinkhorn.1 = (f32[1024,256]{1,0:T(8,128)}, f32[1,1024]{1,0:T(1,128)}, f32[1,2048]{1,0:T(1,128)}) custom-call(bf16[1024,256]{1,0:T(8,128)(2,1)} %xin.1, bf16[2048,512]{1,0:T(8,128)(2,1)} %yin.1, s32[8]{0:T(128)} %nsz.1, s32[8]{0:T(128)} %dsz.1), custom_call_target="tpu_custom_call" | custom-call | tf_op jit(solution)/shard_map/sinkhorn/pallas_call | solution.py:480
  152.2 0.0 copy-start.2
  152.2 0.0 copy-start.1
  152.2 0.0 copy-done
  152.2 2.3 %convert_subtract_fusion = f32[1024,256]{1,0:T(8,128)} fusion(f32[1024,256]{1,0:T(8,128)} %get-tuple-element.6, bf16[1024,256]{1,0:T(8,128)(2,1)S(1)} %copy-done), kind=kLoop, calls=%fused_computation | loop fusion | flops 524288 | bytes 2621440 | tf_op jit(solution)/shard_map/sub | solution.py:536
  154.5 0.0 copy-done.2
  154.6 0.6 copy.9
  155.1 0.0 copy-done.1
  155.1 0.6 copy.10
Async XLA Ops:
  0.6 151.6 %copy-start = (bf16[1024,256]{1,0:T(8,128)(2,1)S(1)}, bf16[1024,256]{1,0:T(8,128)(2,1)}, u32[]{:S(2)}) copy-start(bf16[1024,256]{1,0:T(8,128)(2,1)} %xin.1) | copy-start | bytes 1572868
  152.2 2.3 %copy-start.2 = (f32[1,1024]{1,0:T(1,128)S(1)}, f32[1,1024]{1,0:T(1,128)}, u32[]{:S(2)}) copy-start(f32[1,1024]{1,0:T(1,128)} %get-tuple-element.7) | copy-start | bytes 12292
  152.2 2.9 %copy-start.1 = (f32[1,2048]{1,0:T(1,128)S(1)}, f32[1,2048]{1,0:T(1,128)}, u32[]{:S(2)}) copy-start(f32[1,2048]{1,0:T(1,128)} %get-tuple-element.8) | copy-start | bytes 24580

commit v4 on v3

--- a/solution.py
+++ b/solution.py
@@ -25,7 +25,7 @@
     target, fout, gout,
     X, Y, S, Pm, Wt, NC, F, Fb, avec, bvec, qvec, nvec, qpart, dcvec, cfirst, rfirst, cbuf, rbuf,
     psend, pown, xrecv, zsend, zrecv,
-    local_sem, xg_send, xg_recv, yg_send, yg_recv,
+    local_sem, xg_send, xg_recv, xg_recv2, yg_send, yg_recv,
     cf_send, cf_recv, rf_send, rf_recv, ce_send, ce_recv, re_send, re_recv, px_send, px_recv, pz_send, pz_recv,
 ):
     rows, wc = xin.shape
@@ -114,17 +114,62 @@
         NC[pl.ds(i * T, T), :] = cluster(
             r * rows + i * T + lax.broadcasted_iota(jnp.int32, (T, T), 0), nsz)
 
+    early = XN == 2 and YN == 2 and R == Z
+    half = rows // 2
+
+    def half_copy(block, second, way):
+        peer = {0: c + XN, 1: c - XN, 2: c + 1, 3: c - 1}[way]
+        part = X.at[pl.ds(half if second else 0, half), pl.ds(pl.multiple_of(block * wc, wc), wc)]
+        if second:
+            return rdma(part, part, xg_send.at[block, 4], xg_recv2.at[block], col=peer)
+        return rdma(part, part, xg_send.at[block, way], xg_recv.at[block], col=peer)
+
+    def is_end(dz):
+        return jnp.logical_or(z + dz == 0, z + dz == Z - 1)
+
+    def exists(dz, dx):
+        return jnp.logical_and(
+            jnp.logical_and(z + dz >= 0, z + dz < Z), jnp.logical_and(x + dx >= 0, x + dx < XN))
+
     def take_noise(dz, dx):
-        here = jnp.logical_and(
-            jnp.logical_and(z + dz >= 0, z + dz < Z), jnp.logical_and(x + dx >= 0, x + dx < XN))
+        here = exists(dz, dx)
         block = c + dz * XN + dx
-        pl.when(here)(lambda: noise_copy(block, 0).wait_recv())
+        halves = early and abs(dz) >= 2
         if dx == 0:
+            pl.when(here)(lambda: noise_copy(block, 0).wait_recv())
             noise_send(block, 1 if dz > 0 else 0, here)
-            noise_send(block, 2, here)
-            noise_send(block, 3, here)
-        elif abs(dx) < XN - 1:
-            noise_send(block, 3 if dx > 0 else 2, here)
+            for way in (2, 3):
+                if halves:
+                    ok = jnp.logical_and(here, can_noise(way))
+                    cut = is_end(dz)
+                    send(jnp.logical_and(ok, cut), lambda way=way: half_copy(block, False, way))
+                    send(jnp.logical_and(ok, jnp.logical_not(cut)), lambda way=way: noise_copy(block, way))
+                else:
+                    noise_send(block, way, here)
+        else:
+            if halves:
+                here = jnp.logical_and(here, jnp.logical_not(is_end(dz)))
+            pl.when(here)(lambda: noise_copy(block, 0).wait_recv())
+            if abs(dx) < XN - 1:
+                noise_send(block, 3 if dx > 0 else 2, here)
+            if early and abs(dz) == 1:
+                pass_second(block, dz, jnp.logical_and(here, is_end(dz)))
+
+    def pass_second(block, dz, here):
+        way = 1 if dz > 0 else 0
+        send(jnp.logical_and(here, can_noise(way)), lambda: half_copy(block, True, way))
+
+    def take_second(dz, dx):
+        here = jnp.logical_and(exists(dz, dx), is_end(dz))
+        block = c + dz * XN + dx
+        pl.when(here)(lambda: half_copy(block, True, 0).wait_recv())
+        if abs(dz) < Z - 1:
+            pass_second(block, dz, here)
+
+    def take_first(dz, dx):
+        here = jnp.logical_and(exists(dz, dx), is_end(dz))
+        block = c + dz * XN + dx
+        pl.when(here)(lambda: half_copy(block, False, 0).wait_recv())
 
     def take_data(dy, q):
         here = jnp.logical_and(y + dy >= 0, y + dy < YN)
@@ -155,14 +200,15 @@
 
     quarter = width // Z
     last = PIECES + 1
-    early = XN == 2 and YN == 2 and R == Z
 
     def ready(part, q):
         if not early:
             return jnp.int32(last)
-        noise_step = jnp.abs(part - z) + 1
+        far = jnp.abs(part - z)
+        cut = jnp.logical_and(far == 2, jnp.logical_or(part == 0, part == Z - 1))
+        noise_step = far + 1 + cut.astype(jnp.int32)
         mine = lax.rem(part, CORES) == core
-        data_step = jnp.where(lax.div(part, CORES) == y, 1, jnp.where(mine, q + 1, q + 2))
+        data_step = jnp.where(lax.div(part, CORES) == y, 1, jnp.where(jnp.logical_and(mine, q < PIECES - 1), q + 1, q + 2))
         return jnp.maximum(noise_step, data_step)
 
     def tasks(step):
@@ -190,12 +236,23 @@
         if step < Z:
             for dz in signs(step):
                 take_noise(dz, 0)
-        if step <= PIECES:
+        if step < PIECES:
             for dy in signs(1):
                 take_data(dy, step - 1)
         for dz in signs(step - 1):
             for dx in signs(1):
-                take_noise(dz, dx)
+                if early and step == Z - 1:
+                    take_second(dz, dx)
+                if step < Z or not early:
+                    take_noise(dz, dx)
+        if early and step == Z:
+            for dz in signs(Z - 1):
+                for dx in signs(1):
+                    take_second(dz, dx)
+            for far in range(2, Z):
+                for dz in signs(far):
+                    for dx in signs(1):
+                        take_first(dz, dx)
         if step == 1:
             lx.wait()
             ly.wait()
@@ -206,6 +263,8 @@
                 take_sibling(dy, step - 2)
         if early:
             tasks(step)
+    for dy in signs(1):
+        take_data(dy, PIECES - 1)
     for step in range(2, XN):
         for dz in range(1 - Z, Z):
             for dx in signs(step):
@@ -511,7 +570,8 @@
             pltpu.VMEM((Z - 1, rows, wc), bf16),
             pltpu.VMEM((Z + 1, rows, wc), bf16),
             dma((2,)),
-            dma((C, 4)),
+            dma((C, 5)),
+            dma((C,)),
             dma((C,)),
             dma((R, PIECES, 3)),
             dma((R, PIECES)),

time: 156 us -> 157 us (level)
  no operation moved by 1% of the time
where the time goes in v4:
time: 157 us
  Pallas kernels  153 us (97%)
  other arithmetic  2.3 us (1%)
    pallas_call x1, Pallas kernels, per_device(): pl.pallas_call(functools.partial(kernel, R, C), out_shape=(jax.ShapeDtype...  153 us

profile of v4, /device:TPU:0, one launch (start us, length us, event | category | flops | bytes accessed | tf_op | source)
XLA Modules:
  0.0 157.1 jit_solution(14993040033724121449)
XLA Ops:
  0.6 0.0 copy-start
  0.6 152.9 %sinkhorn.1 = (f32[1024,256]{1,0:T(8,128)}, f32[1,1024]{1,0:T(1,128)}, f32[1,2048]{1,0:T(1,128)}) custom-call(bf16[1024,256]{1,0:T(8,128)(2,1)} %xin.1, bf16[2048,512]{1,0:T(8,128)(2,1)} %yin.1, s32[8]{0:T(128)} %nsz.1, s32[8]{0:T(128)} %dsz.1), custom_call_target="tpu_custom_call" | custom-call | tf_op jit(solution)/shard_map/sinkhorn/pallas_call | solution.py:539
  153.5 0.0 copy-start.2
  153.5 0.0 copy-start.1
  153.6 0.0 copy-done
  153.6 2.3 %convert_subtract_fusion = f32[1024,256]{1,0:T(8,128)} fusion(f32[1024,256]{1,0:T(8,128)} %get-tuple-element.6, bf16[1024,256]{1,0:T(8,128)(2,1)S(1)} %copy-done), kind=kLoop, calls=%fused_computation | loop fusion | flops 524288 | bytes 2621440 | tf_op jit(solution)/shard_map/sub | solution.py:596
  155.9 0.0 copy-done.2
  155.9 0.6 copy.9
  156.5 0.0 copy-done.1
  156.5 0.6 copy.10
Async XLA Ops:
  0.6 152.9 %copy-start = (bf16[1024,256]{1,0:T(8,128)(2,1)S(1)}, bf16[1024,256]{1,0:T(8,128)(2,1)}, u32[]{:S(2)}) copy-start(bf16[1024,256]{1,0:T(8,128)(2,1)} %xin.1) | copy-start | bytes 1572868
  153.5 2.3 %copy-start.2 = (f32[1,1024]{1,0:T(1,128)S(1)}, f32[1,1024]{1,0:T(1,128)}, u32[]{:S(2)}) copy-start(f32[1,1024]{1,0:T(1,128)} %get-tuple-element.7) | copy-start | bytes 12292
  153.5 2.9 %copy-start.1 = (f32[1,2048]{1,0:T(1,128)S(1)}, f32[1,2048]{1,0:T(1,128)}, u32[]{:S(2)}) copy-start(f32[1,2048]{1,0:T(1,128)} %get-tuple-element.8) | copy-start | bytes 24580

commit v5 on v3

--- a/solution.py
+++ b/solution.py
@@ -92,9 +92,8 @@
 
     for way in (0, 1, 2, 3):
         noise_send(c, way, own=True)
-    for q in range(PIECES):
-        for way in (0, 1):
-            data_send(r, q, way, own=True)
+    for way in (0, 1):
+        data_send(r, 0, way, own=True)
     for q in range(PIECES):
         data_send(r, q, 2, own=True)
     lx = pltpu.make_async_copy(xin, noise_part(c), local_sem.at[0])
@@ -193,6 +192,9 @@
         if step <= PIECES:
             for dy in signs(1):
                 take_data(dy, step - 1)
+            if step < PIECES:
+                for way in (0, 1):
+                    data_send(r, step, way, own=True)
         for dz in signs(step - 1):
             for dx in signs(1):
                 take_noise(dz, dx)
@@ -410,7 +412,10 @@
             @pl.when(jnp.logical_or(k > 0, d > 1))
             def _():
                 psend[k, d - 1] = scaled(weighted(zd * XN + lax.rem(x + d, XN)))
-                px_copy(k, d).start()
+
+                @pl.when(k == 0)
+                def _():
+                    px_copy(k, d).start()
 
     @pl.loop(0, Z)
     def _(k):
@@ -433,6 +438,8 @@
         right = zd > z
         more = jnp.logical_or(jnp.logical_and(right, z > 0), jnp.logical_and(zd < z, z < Z - 1))
         total = x_sum(k)
+        for d in range(1, XN):
+            px_copy(k + 1, d).start()
 
         @pl.when(more)
         def _():

time: 156 us -> 159 us (1.019)
  Pallas kernels: 152 us -> 154 us
    pallas_call x1, Pallas kernels: 152 us -> 154 us  [per_device(): pl.pallas_call(functools.partial(kernel, R, C), out_shape=(jax.ShapeDtype...]
where the time goes in v5:
time: 159 us
  Pallas kernels  154 us (97%)
  other arithmetic  2.3 us (1%)
    pallas_call x1, Pallas kernels, per_device(): pl.pallas_call(functools.partial(kernel, R, C), out_shape=(jax.ShapeDtype...  154 us

profile of v5, /device:TPU:0, one launch (start us, length us, event | category | flops | bytes accessed | tf_op | source)
XLA Modules:
  0.0 158.6 jit_solution(1640072349766980856)
XLA Ops:
  0.6 0.0 copy-start
  0.6 154.4 %sinkhorn.1 = (f32[1024,256]{1,0:T(8,128)}, f32[1,1024]{1,0:T(1,128)}, f32[1,2048]{1,0:T(1,128)}) custom-call(bf16[1024,256]{1,0:T(8,128)(2,1)} %xin.1, bf16[2048,512]{1,0:T(8,128)(2,1)} %yin.1, s32[8]{0:T(128)} %nsz.1, s32[8]{0:T(128)} %dsz.1), custom_call_target="tpu_custom_call" | custom-call | tf_op jit(solution)/shard_map/sinkhorn/pallas_call | solution.py:487
  155.0 0.0 copy-start.2
  155.0 0.0 copy-start.1
  155.1 0.0 copy-done
  155.1 2.3 %convert_subtract_fusion = f32[1024,256]{1,0:T(8,128)} fusion(f32[1024,256]{1,0:T(8,128)} %get-tuple-element.6, bf16[1024,256]{1,0:T(8,128)(2,1)S(1)} %copy-done), kind=kLoop, calls=%fused_computation | loop fusion | flops 524288 | bytes 2621440 | tf_op jit(solution)/shard_map/sub | solution.py:543
  157.4 0.0 copy-done.2
  157.4 0.6 copy.9
  158.0 0.0 copy-done.1
  158.0 0.6 copy.10
Async XLA Ops:
  0.6 154.4 %copy-start = (bf16[1024,256]{1,0:T(8,128)(2,1)S(1)}, bf16[1024,256]{1,0:T(8,128)(2,1)}, u32[]{:S(2)}) copy-start(bf16[1024,256]{1,0:T(8,128)(2,1)} %xin.1) | copy-start | bytes 1572868
  155.0 2.3 %copy-start.2 = (f32[1,1024]{1,0:T(1,128)S(1)}, f32[1,1024]{1,0:T(1,128)}, u32[]{:S(2)}) copy-start(f32[1,1024]{1,0:T(1,128)} %get-tuple-element.7) | copy-start | bytes 12292
  155.0 2.9 %copy-start.1 = (f32[1,2048]{1,0:T(1,128)S(1)}, f32[1,2048]{1,0:T(1,128)}, u32[]{:S(2)}) copy-start(f32[1,2048]{1,0:T(1,128)} %get-tuple-element.8) | copy-start | bytes 24580

commit v6 on v3

--- a/solution.py
+++ b/solution.py
@@ -382,77 +382,85 @@
                 part = part + jnp.where(jnp.logical_and(z == at, k == step), value, 0)
         return part
 
-    def weighted(part):
-        return jnp.dot(Wt[...], Y[:, lanes(part, wc)], preferred_element_type=jnp.float32)
-
-    def scaled(v):
-        return jnp.concatenate([v[:, i * T:(i + 1) * T] * F[...] for i in range(wc // T)], axis=1).astype(jnp.bfloat16)
-
-    def px_copy(k, d):
-        return rdma(psend.at[k, d - 1], xrecv.at[k, d - 1], px_send.at[k, d - 1], px_recv.at[k, d - 1],
+    half = rows // 2
+
+    def weighted(part, h):
+        return jnp.dot(Wt[lanes(h, half), :], Y[:, lanes(part, wc)], preferred_element_type=jnp.float32)
+
+    def scaled(v, h):
+        by = F[lanes(h, half), :]
+        return jnp.concatenate([v[:, i * T:(i + 1) * T] * by for i in range(wc // T)], axis=1).astype(jnp.bfloat16)
+
+    def px_copy(k, d, h):
+        return rdma(psend.at[k, d - 1, h], xrecv.at[k, d - 1, h], px_send.at[k, d - 1, h], px_recv.at[k, d - 1, h],
                     col=z * XN + lax.rem(x + d, XN))
 
     def inverse(where, v):
         F[where, :] = 1.0 / v
 
-    head = weighted(order(0) * XN + lax.rem(x + 1, XN))
+    head = weighted(order(0) * XN + lax.rem(x + 1, XN), 0)
     fout[...] = (bvec[...] + nvec[...]) * UNIT
     gout[...] = (avec[...] + qvec[...]) * UNIT
     arrive(*cg(ITERS - 1))
     spread(plain_sum(cbuf, ITERS - 1, C), inverse)
-    psend[0, 0] = scaled(head)
-    px_copy(0, 1).start()
-
-    @pl.loop(0, Z)
-    def _(k):
+    psend[0, 0, 0] = scaled(head, 0)
+    px_copy(0, 1, 0).start()
+
+    @pl.loop(0, Z * 2)
+    def _(n):
+        k, h = lax.div(n, 2), lax.rem(n, 2)
         zd = order(k)
         for d in range(1, XN):
-            @pl.when(jnp.logical_or(k > 0, d > 1))
+            @pl.when(jnp.logical_or(n > 0, d > 1))
             def _():
-                psend[k, d - 1] = scaled(weighted(zd * XN + lax.rem(x + d, XN)))
-                px_copy(k, d).start()
-
-    @pl.loop(0, Z)
-    def _(k):
-        pown[k] = scaled(weighted(order(k) * XN + x))
-
-    def x_sum(k):
+                psend[k, d - 1, h] = scaled(weighted(zd * XN + lax.rem(x + d, XN), h), h)
+                px_copy(k, d, h).start()
+
+    @pl.loop(0, Z * 2)
+    def _(n):
+        k, h = lax.div(n, 2), lax.rem(n, 2)
+        pown[k, h] = scaled(weighted(order(k) * XN + x, h), h)
+
+    def x_sum(k, h):
         for d in range(1, XN):
-            px_copy(k, d).wait_recv()
-        total = pown[k].astype(jnp.float32)
+            px_copy(k, d, h).wait_recv()
+        total = pown[k, h].astype(jnp.float32)
         for d in range(1, XN):
-            total = total + xrecv[k, d - 1].astype(jnp.float32)
+            total = total + xrecv[k, d - 1, h].astype(jnp.float32)
         return total
 
-    def pz_copy(k, to, slot):
-        return rdma(zsend.at[k], zrecv.at[slot], pz_send.at[k], pz_recv.at[slot], col=to * XN + x)
-
-    @pl.loop(0, Z - 1)
-    def _(k):
+    def pz_copy(k, to, slot, h):
+        return rdma(zsend.at[k, h], zrecv.at[slot, h], pz_send.at[k, h], pz_recv.at[slot, h], col=to * XN + x)
+
+    @pl.loop(0, (Z - 1) * 2)
+    def _(n):
+        k, h = lax.div(n, 2), lax.rem(n, 2)
         zd = order(k)
         right = zd > z
         more = jnp.logical_or(jnp.logical_and(right, z > 0), jnp.logical_and(zd < z, z < Z - 1))
-        total = x_sum(k)
+        total = x_sum(k, h)
 
         @pl.when(more)
         def _():
-            pz_copy(k, z, zd).wait_recv()
-            zsend[k] = (total + zrecv[zd].astype(jnp.float32)).astype(jnp.bfloat16)
+            pz_copy(k, z, zd, h).wait_recv()
+            zsend[k, h] = (total + zrecv[zd, h].astype(jnp.float32)).astype(jnp.bfloat16)
 
         @pl.when(jnp.logical_not(more))
         def _():
-            zsend[k] = total.astype(jnp.bfloat16)
+            zsend[k, h] = total.astype(jnp.bfloat16)
 
         to = jnp.where(right, z + 1, z - 1)
         slot = jnp.where(zd == z - 1, Z, zd)
-        pz_copy(k, to, slot).start()
-
-    target[...] = x_sum(Z - 1)
-    for here, slot in ((z > 0, z), (z < Z - 1, Z)):
-        @pl.when(here)
-        def _():
-            pz_copy(0, z, slot).wait_recv()
-            target[...] += zrecv[slot].astype(jnp.float32)
+        pz_copy(k, to, slot, h).start()
+
+    for h in range(2):
+        mine = pl.ds(h * half, half)
+        target[mine, :] = x_sum(Z - 1, h)
+        for here, slot in ((z > 0, z), (z < Z - 1, Z)):
+            @pl.when(here)
+            def _():
+                pz_copy(0, z, slot, h).wait_recv()
+                target[mine, :] += zrecv[slot, h].astype(jnp.float32)
 
     for cond, make in sent:
         pl.when(cond)(lambda make=make: make().wait_send())
@@ -462,9 +470,11 @@
             copy.wait_send()
     for k in range(Z):
         for d in range(1, XN):
-            px_copy(k, d).wait_send()
+            for h in range(2):
+                px_copy(k, d, h).wait_send()
     for k in range(Z - 1):
-        pz_copy(k, z, 0).wait_send()
+        for h in range(2):
+            pz_copy(k, z, 0, h).wait_send()
 
 
 def per_device(R, C, noise_latents, data_latents, noise_sizes, data_sizes):
@@ -505,11 +515,11 @@
             pltpu.VMEM((1, R, 2, cols), f32),
             pltpu.VMEM((ITERS, C, 1, rows), f32),
             pltpu.VMEM((ITERS - 1, R, 1, cols), f32),
-            pltpu.VMEM((Z, XN - 1, rows, wc), bf16),
-            pltpu.VMEM((Z, rows, wc), bf16),
-            pltpu.VMEM((Z, XN - 1, rows, wc), bf16),
-            pltpu.VMEM((Z - 1, rows, wc), bf16),
-            pltpu.VMEM((Z + 1, rows, wc), bf16),
+            pltpu.VMEM((Z, XN - 1, 2, rows // 2, wc), bf16),
+            pltpu.VMEM((Z, 2, rows // 2, wc), bf16),
+            pltpu.VMEM((Z, XN - 1, 2, rows // 2, wc), bf16),
+            pltpu.VMEM((Z - 1, 2, rows // 2, wc), bf16),
+            pltpu.VMEM((Z + 1, 2, rows // 2, wc), bf16),
             dma((2,)),
             dma((C, 4)),
             dma((C,)),
@@ -523,10 +533,10 @@
             dma((ITERS, C)),
             dma((ITERS - 1, R - 1)),
             dma((ITERS - 1, R)),
-            dma((Z, XN - 1)),
-            dma((Z, XN - 1)),
-            dma((Z - 1,)),
-            dma((Z + 1,)),
+            dma((Z, XN - 1, 2)),
+            dma((Z, XN - 1, 2)),
+            dma((Z - 1, 2)),
+            dma((Z + 1, 2)),
         ],
         compiler_params=pltpu.CompilerParams(
             collective_id=0, has_side_effects=True, vmem_limit_bytes=58 * 1024 * 1024

time: 156 us -> 156 us (level)
  no operation moved by 1% of the time
where the time goes in v6:
time: 156 us
  Pallas kernels  152 us (97%)
  other arithmetic  2.3 us (1%)
    pallas_call x1, Pallas kernels, per_device(): pl.pallas_call(functools.partial(kernel, R, C), out_shape=(jax.ShapeDtype...  152 us

profile of v6, /device:TPU:0, one launch (start us, length us, event | category | flops | bytes accessed | tf_op | source)
XLA Modules:
  0.0 155.8 jit_solution(8260811992812342118)
XLA Ops:
  0.6 0.0 copy-start
  0.6 151.6 %sinkhorn.1 = (f32[1024,256]{1,0:T(8,128)}, f32[1,1024]{1,0:T(1,128)}, f32[1,2048]{1,0:T(1,128)}) custom-call(bf16[1024,256]{1,0:T(8,128)(2,1)} %xin.1, bf16[2048,512]{1,0:T(8,128)(2,1)} %yin.1, s32[8]{0:T(128)} %nsz.1, s32[8]{0:T(128)} %dsz.1), custom_call_target="tpu_custom_call" | custom-call | tf_op jit(solution)/shard_map/sinkhorn/pallas_call | solution.py:490
  152.3 0.0 copy-start.2
  152.3 0.0 copy-start.1
  152.3 0.0 copy-done
  152.3 2.3 %convert_subtract_fusion = f32[1024,256]{1,0:T(8,128)} fusion(f32[1024,256]{1,0:T(8,128)} %get-tuple-element.6, bf16[1024,256]{1,0:T(8,128)(2,1)S(1)} %copy-done), kind=kLoop, calls=%fused_computation | loop fusion | flops 524288 | bytes 2621440 | tf_op jit(solution)/shard_map/sub | solution.py:546
  154.6 0.0 copy-done.2
  154.6 0.6 copy.9
  155.2 0.0 copy-done.1
  155.2 0.6 copy.10
Async XLA Ops:
  0.6 151.7 %copy-start = (bf16[1024,256]{1,0:T(8,128)(2,1)S(1)}, bf16[1024,256]{1,0:T(8,128)(2,1)}, u32[]{:S(2)}) copy-start(bf16[1024,256]{1,0:T(8,128)(2,1)} %xin.1) | copy-start | bytes 1572868
  152.3 2.3 %copy-start.2 = (f32[1,1024]{1,0:T(1,128)S(1)}, f32[1,1024]{1,0:T(1,128)}, u32[]{:S(2)}) copy-start(f32[1,1024]{1,0:T(1,128)} %get-tuple-element.7) | copy-start | bytes 12292
  152.3 2.9 %copy-start.1 = (f32[1,2048]{1,0:T(1,128)S(1)}, f32[1,2048]{1,0:T(1,128)}, u32[]{:S(2)}) copy-start(f32[1,2048]{1,0:T(1,128)} %get-tuple-element.8) | copy-start | bytes 24580
